TPU v7x, 32 devices: a whole 2x2x4 slice. The times are simulated.
32 devices in a mesh: bus: 8 (over z, y), line: 4 (over x, core).
Axes of the slice: x: 2, y: 2, z: 4, core: 2. Of those that a mesh axis runs over, the one named last changes fastest.
Arguments:
- generation: bfloat16 [512, 16384], P(None, 'bus'), may hold values from -6 to 6
- profiles: float32 [24, 16384], P(None, 'bus'), may hold values from -5 to 5
- scen_profile: int32 [512], replicated, may hold values from 0 to 23
- ptdf: bfloat16 [16384, 16384], P('line', 'bus'), may hold values from -0.046875 to 0.046875
- lodf: float32 [1536, 512], P('line'), may hold values from -1 to 1
- limits: float32 [1536], P('line'), may hold values from 0.5 to 2
- monitored: int32 [1536], P('line'), may hold values from 0 to 16383, as said below
- outages: int32 [512], replicated, may hold values from 0 to 16383, as said below
- cost_quad: float32 [16384], P('bus'), may hold values from 0.5 to 2
Outputs:
- gradient: bfloat16 [512, 16384], P('line', 'bus')
- outage_flow: float32 [512, 512], P('bus')
- outage_sens: float32 [512, 512], P('bus')
Inputs may be any that keep to these rules, and one draw needn't show every extreme that they name: `monitored`: the entries with positions k * 384 to (k + 1) * 384 - 1 are distinct line ids of the k-th block of 4096 lines (ids k * 4096 to (k + 1) * 4096 - 1). `outages`: distinct line ids; how many fall in each block of 4096 lines varies from block to block.
All inputs are finite; a program needn't handle non-finite values.
Results may differ from a plain program's by a relative error of at most 0.0029.
Values may be sent and summed in bfloat16 or wider, within the bound.
A program may use at most 64 MiB of HBM per device.

v0:
```python
import math

import jax
import jax.numpy as jnp
from jax import lax
from jax.sharding import PartitionSpec as P

sharpness = 4.0


def contingency(pieces, lodf, limits, outage_total):
    base_block, outage_block = pieces
    post_flow = base_block[:, :, None] + lodf[None, :, :] * outage_block[:, None, :]
    bounds = limits[None, :, None]
    raw_slope = jax.nn.sigmoid(sharpness * (post_flow - bounds)) - jax.nn.sigmoid(
        sharpness * (-post_flow - bounds)
    )
    direct = jnp.sum(raw_slope, axis=2) / outage_total
    sens_part = jnp.einsum("smk,mk->sk", raw_slope, lodf, precision=lax.Precision.HIGHEST)
    return (direct, sens_part)


def on_device(
    generation, profiles, scen_profile, ptdf, lodf, limits, monitored, outages, cost_quad
):
    profile_count = profiles.shape[0]
    profile_pick = (
        scen_profile[:, None] == jnp.arange(profile_count, dtype=jnp.int32)[None, :]
    ).astype(jnp.float32)
    loads = jnp.dot(profile_pick, profiles, precision=lax.Precision.HIGHEST)
    injection = (generation.astype(jnp.float32) - loads).astype(jnp.bfloat16)
    scen_rows = injection.shape[0] // lax.axis_size("bus")
    line_rows = ptdf.shape[0]
    first_line = lax.axis_index("line") * line_rows
    local_monitored = monitored - first_line
    positions = jnp.arange(line_rows, dtype=jnp.int32)
    picker = ((outages - first_line)[None, :] == positions[:, None]).astype(jnp.float32)
    monitor_count = monitored.shape[0]
    watched_rows = jnp.take(ptdf, local_monitored, axis=0)
    outage_rows = jnp.dot(
        picker.T.astype(jnp.bfloat16), ptdf, preferred_element_type=jnp.float32
    ).astype(jnp.bfloat16)
    used_rows = jnp.concatenate([watched_rows, outage_rows], axis=0)
    inputs = injection
    compact = lax.psum_scatter(
        lax.dot_general(
            inputs, used_rows, (((1,), (1,)), ((), ())), preferred_element_type=jnp.float32
        ),
        "bus",
        scatter_dimension=0,
        tiled=True,
    )
    base = compact[:, :monitor_count]
    outflow = lax.psum(compact[:, monitor_count:], "line")
    outage_total = outages.shape[0]
    monitored_total = monitor_count * lax.axis_size("line")
    block_size = math.gcd(scen_rows, 4)
    base_blocks = base.reshape(scen_rows // block_size, block_size, monitor_count)
    outage_blocks = outflow.reshape(scen_rows // block_size, block_size, outage_total)
    direct, sens_part = lax.map(
        lambda pieces: contingency(pieces, lodf, limits, outage_total), (base_blocks, outage_blocks)
    )
    direct = direct.reshape(scen_rows, monitor_count)
    sens_part = sens_part.reshape(scen_rows, outage_total)
    sens_total = lax.psum(sens_part, "line")
    backward = sens_total / outage_total
    outage_sens = sens_total / math.sqrt(monitored_total)
    adjoint = jnp.zeros((scen_rows, line_rows), jnp.float32).at[:, local_monitored].add(direct)
    adjoint = adjoint + jnp.dot(backward, picker.T, precision=lax.Precision.HIGHEST)
    adjoint_half = adjoint.astype(jnp.bfloat16)
    all_adjoint = lax.all_gather(adjoint_half, "bus", axis=0, tiled=True)
    grad_rows = all_adjoint.shape[0] // lax.axis_size("line")
    inputs = all_adjoint
    pushed = lax.psum_scatter(
        jnp.dot(inputs, ptdf, preferred_element_type=jnp.float32),
        "line",
        scatter_dimension=0,
        tiled=True,
    )
    own_generation = lax.dynamic_slice_in_dim(
        generation, lax.axis_index("line") * grad_rows, grad_rows, 0
    ).astype(jnp.float32)
    gradient = (cost_quad[None, :] * own_generation + pushed).astype(jnp.bfloat16)
    return (gradient, outflow, outage_sens)


def solution(mesh):
    placed = (
        P(None, "bus"),
        P(None, "bus"),
        P(),
        P("line", "bus"),
        P("line", None),
        P("line"),
        P("line"),
        P(),
        P("bus"),
    )
    return jax.shard_map(
        on_device,
        mesh=mesh,
        in_specs=placed,
        out_specs=(P("line", "bus"), P("bus", None), P("bus", None)),
        check_vma=False,
    )
```

profile of v0, /device:TPU:30, one launch (start us, length us, event | category | flops | bytes accessed | tf_op | source)
XLA Modules:
  0.0 393.5 jit_solution(11234473996081402012)
XLA Ops:
  8.6 12.3 %gather_fusion = bf16[384,2048]{1,0:T(8,128)(2,1)S(1)} fusion(bf16[4096,2048]{1,0:T(8,128)(2,1)} %param.14, s32[1024]{0:T(1024)S(1)} %pad_clamp_fusion), kind=kCustom, calls=%fused_computation | custom fusion | bytes 3147264 | tf_op jit(solution)/shard_map/jit(_take)/gather | solution.py:39
  21.0 12.5 %fusion.9 = bf16[512,2048]{1,0:T(8,128)(2,1)S(1)} fusion(bf16[4096,2048]{1,0:T(8,128)(2,1)} %param.14, s32[512]{0:T(512)S(1)} %broadcast_subtract_fusion), kind=kOutput, calls=%fused_computation.21 | convolution fusion | flops 8597274624 | bytes 18876416 | tf_op jit(solution)/shard_map/dot_general | solution.py:40
  37.1 3.6 fusion.5
  40.8 64.9 %reduce-scatter.3.cloned.1.call-done = f32[64,896]{1,0:T(8,128)} async-done(((f32[512,896]{1,0:T(8,128)}), f32[64,896]{1,0:T(8,128)}) %reduce-scatter.3.cloned.1.call-update) | async-done | bytes 229392 | tf_op jit(solution)/shard_map/reduce_scatter | solution.py:45
  108.5 31.7 %all-reduce.3.cloned.1.call-done = f32[64,512]{1,0:T(8,128)} async-done(((f32[64,512]{1,0:T(8,128)}), f32[64,512]{1,0:T(8,128)}) %all-reduce.3.cloned.1.call-update) | async-done | bytes 131088 | tf_op jit(solution)/shard_map/psum | solution.py:54
  141.2 70.0 %while.12 = (s32[]{:T(128)}, f32[16,4,384]{2,1,0:T(4,128)S(1)}, f32[16,4,512]{2,1,0:T(4,128)S(1)}, f32[16,4,384]{2,1,0:T(4,128)S(1)}, f32[384,512]{1,0:T(8,128)S...) while((s32[]{:T(128)}, f32[16,4,384]{2,1,0:T(4,128)S(1)}, f32[16,4,512]{2,1,0:T(4,128)S(1)}, ...), condition=%wide.region_4.5_spmd, body=%wide.region_2.4_spmd.sunk | while | flops 24377344 | bytes 2462829 | solution.py:60
  141.2 2.2 fusion.24
  145.6 2.2 fusion.24
  147.8 2.1 multiply_reduce_fusion.2
  150.0 2.2 fusion.24
  154.4 2.2 fusion.24
  156.6 2.1 multiply_reduce_fusion.2
  158.7 2.2 fusion.24
  160.9 2.1 multiply_reduce_fusion.2
  163.1 2.2 fusion.24
  167.5 2.2 fusion.24
  171.9 2.2 fusion.24
  176.3 2.2 fusion.24
  180.6 2.2 fusion.24
  185.0 2.2 fusion.24
  189.4 2.2 fusion.24
  193.8 2.2 fusion.24
  198.1 2.2 fusion.24
  202.5 2.2 fusion.24
  206.9 2.2 fusion.24
  212.2 31.3 %all-reduce.5.cloned.1.call-done = f32[64,512]{1,0:T(8,128)} async-done(((f32[64,512]{1,0:T(8,128)}), f32[64,512]{1,0:T(8,128)}) %all-reduce.5.cloned.1.call-update) | async-done | bytes 131088 | tf_op jit(solution)/shard_map/psum | solution.py:65
  243.5 4.5 %fusion.1 = f32[64,4096]{0,1:T(8,128)S(1)} fusion(s32[512]{0:T(512)S(1)} %broadcast_subtract_fusion, f32[64,512]{1,0:T(8,128)} %all-reduce.5.cloned.1.call-done), kind=kOutput, calls=%fused_computation.12 | convolution fusion | flops 1612742656 | bytes 1181696 | tf_op jit(solution)/shard_map/dot_general | solution.py:69
  248.0 3.4 scatter_custom_fusion
  252.6 71.8 %all-gather.2.cloned.1.call-done = bf16[512,4096]{1,0:T(8,128)(2,1)} async-done(((bf16[64,4096]{1,0:T(8,128)(2,1)}), bf16[512,4096]{1,0:T(8,128)(2,1)}) %all-gather.2.cloned.1.call-update) | async-done | bytes 4194320 | tf_op jit(solution)/shard_map/all_gather | solution.py:71
  324.4 15.0 %fusion.17 = f32[512,2048]{1,0:T(8,128)} fusion(bf16[512,4096]{1,0:T(8,128)(2,1)} %all-gather.2.cloned.1.call-done, bf16[4096,2048]{1,0:T(8,128)(2,1)} %param.14), kind=kOutput, calls=%fused_computation.37 | convolution fusion | flops 8589934592 | bytes 25165824 | tf_op jit(solution)/shard_map/dot_general | solution.py:75
  340.9 43.1 %reduce-scatter.5.cloned.1.call-done = f32[128,2048]{1,0:T(8,128)} async-done(((f32[512,2048]{1,0:T(8,128)}), f32[128,2048]{1,0:T(8,128)}) %reduce-scatter.5.cloned.1.call-update) | async-done | bytes 1048592 | tf_op jit(solution)/shard_map/reduce_scatter | solution.py:74
  384.1 2.3 add_convert_fusion
  (120 shorter events, 41.1 us)
Async XLA Ops:
  7.2 26.5 %copy-start = (f32[24,2048]{1,0:T(8,128)S(1)}, f32[24,2048]{1,0:T(8,128)}, u32[]{:S(2)}) copy-start(f32[24,2048]{1,0:T(8,128)} %param.12) | copy-start | bytes 589828
  7.2 98.6 %reduce-scatter.3.cloned.1.call-start = ((), (), s32[]{:S(2)}) async-start(), calls=%async_computation.2 | async-start | bytes 2064384 | tf_op jit(solution)/shard_map/reduce_scatter | solution.py:45
  33.4 1.6 copy-start.1
  33.5 1.6 copy-start.5
  37.1 104.1 %copy-start.6 = (f32[384,512]{1,0:T(8,128)S(1)}, f32[384,512]{1,0:T(8,128)}, u32[]{:S(2)}) copy-start(f32[384,512]{1,0:T(8,128)} %param.15) | copy-start | bytes 2359300
  37.1 104.1 %copy-start.7 = (f32[384]{0:T(512)S(1)}, f32[384]{0:T(512)}, u32[]{:S(2)}) copy-start(f32[384]{0:T(512)} %param.16) | copy-start | bytes 4612
  40.8 99.5 %all-reduce.3.cloned.1.call-start = ((), (), s32[]{:S(2)}) async-start(), calls=%async_computation.3 | async-start | bytes 262144 | tf_op jit(solution)/shard_map/psum | solution.py:54
  107.3 136.2 %all-reduce.5.cloned.1.call-start = ((), (), s32[]{:S(2)}) async-start(), calls=%async_computation.4 | async-start | bytes 262144 | tf_op jit(solution)/shard_map/psum | solution.py:65
  212.0 112.4 %all-gather.2.cloned.1.call-start = ((), (), s32[]{:S(2)}) async-start(), calls=%async_computation.5 | async-start | bytes 4718592 | tf_op jit(solution)/shard_map/all_gather | solution.py:71
  252.5 131.5 %reduce-scatter.5.cloned.1.call-start = ((), (), s32[]{:S(2)}) async-start(), calls=%async_computation.6 | async-start | bytes 5242880 | tf_op jit(solution)/shard_map/reduce_scatter | solution.py:74
  339.4 0.9 copy-start.3
  339.4 44.7 %copy-start.4 = (f32[2048]{0:T(1024)S(1)}, f32[2048]{0:T(1024)}, u32[]{:S(2)}) copy-start(f32[2048]{0:T(1024)} %param.19) | copy-start | bytes 24580
  339.4 47.0 %copy-start.2 = (f32[64,512]{1,0:T(8,128)S(1)}, f32[64,512]{1,0:T(8,128)}, u32[]{:S(2)}) copy-start(f32[64,512]{1,0:T(8,128)} %all-reduce.3.cloned.1.call-done) | copy-start | bytes 393220
Sparse Core Ops, SparseCore 0:
  40.9 64.8 reduce-scatter.2
  108.7 31.4 all-reduce.2
  212.1 31.3 all-reduce.4
  252.6 71.6 all-gather.1
  339.5 44.5 reduce-scatter.4
where the time goes:
time: 397 us; the launch traced here: 394 us
  waiting for transfers between devices  243 us (61%)
  other arithmetic  76.8 us (19%)
  matrix products  37.6 us (9%)
  local copies, waits for them, and re-layouts  21.1 us (5%)
  between operations  13.9 us (4%)
    all_gather x1, waiting for transfers between devices, on_device(): all_adjoint = lax.all_gather(adjoint_half, 'bus', axis=0, tiled=True)  71.8 us
    reduce_scatter x1, waiting for transfers between devices, on_device(): lax.psum_scatter(lax.dot_general(inputs, used_rows, (((1,), (1,)), ((), (...  64.9 us
    reduce_scatter x1, waiting for transfers between devices, on_device(): lax.psum_scatter(jnp.dot(inputs, ptdf, preferred_element_type=jnp.float32...  43.1 us
    reduce_sum x16, other arithmetic, contingency(): direct = jnp.sum(raw_slope, axis=2) / outage_total  35.1 us
    dot_general x16, other arithmetic, contingency(): jnp.einsum('smk,mk->sk', raw_slope, lodf, precision=lax.Precision.HIGHEST)  33.5 us
    psum x1, waiting for transfers between devices, on_device(): outflow = lax.psum(compact[:, monitor_count:], 'line')  31.7 us
    psum x1, waiting for transfers between devices, on_device(): sens_total = lax.psum(sens_part, 'line')  31.3 us
    dot_general x1, matrix products, on_device(): jnp.dot(inputs, ptdf, preferred_element_type=jnp.float32)  15 us
  transfers between devices with their start and end apart: 5, of which 5 were waited for; matrix products, arithmetic and copies ran while one was open for 0% of the time, Pallas kernels for 0%

commit v1 on v0

v1 whole, which is shorter than its diff:
```python
import functools
import math

import jax
import jax.numpy as jnp
from jax import lax
from jax.experimental import pallas as pl
from jax.experimental.pallas import tpu as pltpu
from jax.sharding import PartitionSpec as P

MESH = pl.DeviceIdType.MESH
HIGH = lax.Precision.HIGHEST
ROWS_DOT = (((1,), (1,)), ((), ()))
LANES = 128


def remote(src, dst, send_sem, recv_sem, axis, peer):
    return pltpu.make_async_remote_copy(
        src_ref=src,
        dst_ref=dst,
        send_sem=send_sem,
        recv_sem=recv_sem,
        device_id={axis: peer},
        device_id_type=MESH,
    )


def step_kernel(
    n_bus,
    n_line,
    inj_ref,
    rows_ref,
    lodf_ref,
    limits_ref,
    monitored_ref,
    outages_ref,
    keep_ref,
    generation_ref,
    cost_ref,
    gradient_ref,
    outflow_ref,
    sens_ref,
    out_part,
    out_got,
    out_sum,
    mon_part,
    mon_got,
    outbus_got,
    out_all,
    base_t,
    limit_wide,
    direct_t,
    flow2,
    sens_tall,
    sens_part,
    sens_got,
    adjoint,
    core_part,
    core_got,
    own_part,
    hi_send,
    hi_got,
    line_send,
    line_recv,
    mon_send,
    mon_recv,
    ob_send,
    ob_recv,
    oa_send,
    oa_recv,
    se_send,
    se_recv,
    ad_send,
    ad_recv,
    co_send,
    co_recv,
    hi_ssem,
    hi_rsem,
):
    scen, buses = inj_ref.shape
    count_m, count_k = lodf_ref.shape
    own = scen // n_bus
    width = count_k // n_line
    grad_rows = scen // n_line
    n_hi = n_line // 2
    b = lax.axis_index("bus")
    l = lax.axis_index("line")

    barrier = pltpu.get_barrier_semaphore()
    for d in range(1, n_bus):
        pl.semaphore_signal(
            barrier, inc=1, device_id={"bus": lax.rem(b + d, n_bus)}, device_id_type=MESH
        )
    for d in range(1, n_line):
        pl.semaphore_signal(
            barrier, inc=1, device_id={"line": lax.rem(l + d, n_line)}, device_id_type=MESH
        )
    for j in range(n_line):
        out_part[j] = lax.dot_general(
            inj_ref[...],
            rows_ref[count_m + j * width : count_m + (j + 1) * width, :],
            ROWS_DOT,
            preferred_element_type=jnp.float32,
        )
    pl.semaphore_wait(barrier, n_bus + n_line - 2)
    line_copies = []
    for d in range(1, n_line):
        peer = lax.rem(l + d, n_line)
        copy = remote(
            out_part.at[peer], out_got.at[d - 1], line_send.at[d - 1], line_recv.at[d - 1], "line", peer
        )
        copy.start()
        line_copies.append(copy)
    mon_part[...] = lax.dot_general(
        inj_ref[...], rows_ref[:count_m, :], ROWS_DOT, preferred_element_type=jnp.float32
    )
    mon_copies = []
    for d in range(1, n_bus):
        peer = lax.rem(b + d, n_bus)
        copy = remote(
            mon_part.at[pl.ds(pl.multiple_of(peer * own, own), own), :],
            mon_got.at[d - 1],
            mon_send.at[d - 1],
            mon_recv.at[d - 1],
            "bus",
            peer,
        )
        copy.start()
        mon_copies.append(copy)
    limit_wide[...] = jnp.broadcast_to(2.0 * limits_ref[...], limit_wide.shape)
    for copy in line_copies:
        copy.wait()
    total = out_part[l]
    for d in range(1, n_line):
        total = total + out_got[d - 1]
    out_sum[...] = total
    ob_copies = []
    for d in range(1, n_bus):
        peer = lax.rem(b + d, n_bus)
        copy = remote(
            out_sum.at[pl.ds(pl.multiple_of(peer * own, own), own), :],
            outbus_got.at[d - 1],
            ob_send.at[d - 1],
            ob_recv.at[d - 1],
            "bus",
            peer,
        )
        copy.start()
        ob_copies.append(copy)
    own_rows = pl.ds(pl.multiple_of(b * own, own), own)
    for copy in mon_copies:
        copy.wait()
    base = mon_part[own_rows, :]
    for d in range(1, n_bus):
        base = base + mon_got[d - 1]
    spread = jnp.concatenate([2.0 * base, jnp.zeros((LANES - own, count_m), jnp.float32)], axis=0)
    base_t[...] = spread.T
    for copy in ob_copies:
        copy.wait()
    flow = out_sum[own_rows, :]
    for d in range(1, n_bus):
        flow = flow + outbus_got[d - 1]
    out_all[l] = flow
    oa_copies = []
    for d in range(1, n_line):
        peer = lax.rem(l + d, n_line)
        copy = remote(
            out_all.at[l], out_all.at[l], oa_send.at[d - 1], oa_recv.at[d - 1], "line", peer
        )
        copy.start()
        oa_copies.append(copy)
    direct_t[...] = jnp.zeros_like(direct_t)
    for copy in oa_copies:
        copy.wait()
    flows = jnp.concatenate([out_all[j] for j in range(n_line)], axis=1)
    outflow_ref[...] = flows
    flow2[...] = jnp.broadcast_to((2.0 * flows)[:, None, :], flow2.shape)

    lane = lax.broadcasted_iota(jnp.int32, (8, LANES), 1)
    group = 8
    k_tiles = count_k // LANES

    def one_scenario(s, carry):
        mine = lane == s
        flow_rows = [
            flow2[s, :, t * LANES : (t + 1) * LANES] for t in range(k_tiles)
        ]

        def some_lines(g, sums):
            sums = list(sums)
            for i in range(group):
                start = pl.multiple_of((g * group + i) * 8, 8)
                here = pl.ds(start, 8)
                column = jnp.sum(jnp.where(mine, base_t[here, :], 0.0), axis=1, keepdims=True)
                limit = limit_wide[here, :]
                low = column - limit
                high = column + limit
                along = jnp.zeros((8, LANES), jnp.float32)
                for t in range(k_tiles):
                    factor = lodf_ref[here, t * LANES : (t + 1) * LANES]
                    change = factor * flow_rows[t]
                    slope = jnp.tanh(change + low) + jnp.tanh(change + high)
                    along = along + slope
                    sums[t] = sums[t] + factor * slope
                direct = jnp.sum(along, axis=1, keepdims=True)
                direct_t[here, :] = jnp.where(mine, direct, direct_t[here, :])
            return tuple(sums)

        sums = lax.fori_loop(
            0,
            count_m // (8 * group),
            some_lines,
            tuple(jnp.zeros((8, LANES), jnp.float32) for _ in range(k_tiles)),
        )
        for t in range(k_tiles):
            sens_tall[s, :, t * LANES : (t + 1) * LANES] = sums[t]
        return carry

    lax.fori_loop(0, own, one_scenario, 0)
    sens_part[...] = 0.5 * jnp.sum(sens_tall[...], axis=1)
    sens_got[l] = sens_part[...]
    se_copies = []
    for d in range(1, n_line):
        peer = lax.rem(l + d, n_line)
        copy = remote(
            sens_part, sens_got.at[l], se_send.at[d - 1], se_recv.at[d - 1], "line", peer
        )
        copy.start()
        se_copies.append(copy)
    direct = direct_t[...].T[:own, :] * (0.5 / count_k)
    match = (monitored_ref[...] == outages_ref[...]).astype(jnp.float32)
    for copy in se_copies:
        copy.wait()
    total = sens_got[0]
    for j in range(1, n_line):
        total = total + sens_got[j]
    sens_ref[...] = total * (1.0 / math.sqrt(count_m * n_line))
    backward = total * (1.0 / count_k)
    direct = direct + lax.dot_general(
        backward, match, ROWS_DOT, precision=HIGH, preferred_element_type=jnp.float32
    )
    adjoint[own_rows, :count_m] = direct.astype(jnp.bfloat16)
    adjoint[own_rows, count_m:] = (backward * keep_ref[...]).astype(jnp.bfloat16)
    ad_copies = []
    for d in range(1, n_bus):
        peer = lax.rem(b + d, n_bus)
        copy = remote(
            adjoint.at[own_rows, :],
            adjoint.at[own_rows, :],
            ad_send.at[d - 1],
            ad_recv.at[d - 1],
            "bus",
            peer,
        )
        copy.start()
        ad_copies.append(copy)
    for copy in ad_copies:
        copy.wait()

    core = lax.rem(l, 2)
    hi = l // 2
    pair = l + 1 - 2 * core
    core_copies = []
    for h in range(n_hi):
        rows = pl.ds(pl.multiple_of((2 * h + 1 - core) * grad_rows, grad_rows), grad_rows)
        core_part[h] = jnp.dot(adjoint[rows, :], rows_ref[...], preferred_element_type=jnp.float32)
        copy = remote(core_part.at[h], core_got.at[h], co_send.at[h], co_recv.at[h], "line", pair)
        copy.start()
        core_copies.append(copy)
    for h in range(n_hi):
        rows = pl.ds(pl.multiple_of((2 * h + core) * grad_rows, grad_rows), grad_rows)
        own_part[h] = jnp.dot(adjoint[rows, :], rows_ref[...], preferred_element_type=jnp.float32)
    for copy in core_copies:
        copy.wait()
    hi_copies = []
    for d in range(1, n_hi):
        other = lax.rem(hi + d, n_hi)
        hi_send[d - 1] = (own_part[other] + core_got[other]).astype(jnp.bfloat16)
        copy = remote(
            hi_send.at[d - 1],
            hi_got.at[d - 1],
            hi_ssem.at[d - 1],
            hi_rsem.at[d - 1],
            "line",
            2 * other + core,
        )
        copy.start()
        hi_copies.append(copy)
    mine = pl.ds(pl.multiple_of(l * grad_rows, grad_rows), grad_rows)
    total = own_part[hi] + core_got[hi]
    total = total + cost_ref[...] * generation_ref[mine, :].astype(jnp.float32)
    for copy in hi_copies:
        copy.wait()
    for d in range(1, n_hi):
        total = total + hi_got[d - 1].astype(jnp.float32)
    gradient_ref[...] = total.astype(jnp.bfloat16)


def on_device(
    n_bus, n_line, generation, profiles, scen_profile, ptdf, lodf, limits, monitored, outages, cost_quad
):
    profile_count = profiles.shape[0]
    profile_pick = (
        scen_profile[:, None] == jnp.arange(profile_count, dtype=jnp.int32)[None, :]
    ).astype(jnp.float32)
    loads = jnp.dot(profile_pick, profiles, precision=HIGH)
    injection = (generation.astype(jnp.float32) - loads).astype(jnp.bfloat16)
    line_rows = ptdf.shape[0]
    scen, buses = injection.shape
    count_m, count_k = lodf.shape
    first_line = lax.axis_index("line") * line_rows
    local_outages = outages - first_line
    local_monitored = monitored - first_line
    positions = jnp.arange(line_rows, dtype=jnp.int32)
    picker = (local_outages[:, None] == positions[None, :]).astype(jnp.bfloat16)
    watched_rows = jnp.take(ptdf, local_monitored, axis=0, mode="clip")
    outage_rows = jnp.dot(picker, ptdf, preferred_element_type=jnp.float32).astype(jnp.bfloat16)
    used_rows = jnp.concatenate([watched_rows, outage_rows], axis=0)
    seen = jnp.any(monitored[:, None] == outages[None, :], axis=0)
    keep = (local_outages >= 0) & (local_outages < line_rows) & jnp.logical_not(seen)
    keep = keep.astype(jnp.float32)[None, :]

    own = scen // n_bus
    width = count_k // n_line
    grad_rows = scen // n_line
    n_hi = n_line // 2
    vmem = pl.BlockSpec(memory_space=pltpu.VMEM)
    f32 = jnp.float32
    bf16 = jnp.bfloat16
    dma = pltpu.SemaphoreType.DMA
    return pl.pallas_call(
        functools.partial(step_kernel, n_bus, n_line),
        out_shape=(
            jax.ShapeDtypeStruct((grad_rows, buses), bf16),
            jax.ShapeDtypeStruct((own, count_k), f32),
            jax.ShapeDtypeStruct((own, count_k), f32),
        ),
        in_specs=[vmem] * 9,
        out_specs=(vmem, vmem, vmem),
        scratch_shapes=[
            pltpu.VMEM((n_line, scen, width), f32),
            pltpu.VMEM((n_line - 1, scen, width), f32),
            pltpu.VMEM((scen, width), f32),
            pltpu.VMEM((scen, count_m), f32),
            pltpu.VMEM((n_bus - 1, own, count_m), f32),
            pltpu.VMEM((n_bus - 1, own, width), f32),
            pltpu.VMEM((n_line, own, width), f32),
            pltpu.VMEM((count_m, LANES), f32),
            pltpu.VMEM((count_m, LANES), f32),
            pltpu.VMEM((count_m, LANES), f32),
            pltpu.VMEM((own, 8, count_k), f32),
            pltpu.VMEM((own, 8, count_k), f32),
            pltpu.VMEM((own, count_k), f32),
            pltpu.VMEM((n_line, own, count_k), f32),
            pltpu.VMEM((scen, count_m + count_k), bf16),
            pltpu.VMEM((n_hi, grad_rows, buses), f32),
            pltpu.VMEM((n_hi, grad_rows, buses), f32),
            pltpu.VMEM((n_hi, grad_rows, buses), f32),
            pltpu.VMEM((n_hi - 1, grad_rows, buses), bf16),
            pltpu.VMEM((n_hi - 1, grad_rows, buses), bf16),
            dma((n_line - 1,)),
            dma((n_line - 1,)),
            dma((n_bus - 1,)),
            dma((n_bus - 1,)),
            dma((n_bus - 1,)),
            dma((n_bus - 1,)),
            dma((n_line - 1,)),
            dma((n_line - 1,)),
            dma((n_line - 1,)),
            dma((n_line - 1,)),
            dma((n_bus - 1,)),
            dma((n_bus - 1,)),
            dma((n_hi,)),
            dma((n_hi,)),
            dma((n_hi - 1,)),
            dma((n_hi - 1,)),
        ],
        compiler_params=pltpu.CompilerParams(
            collective_id=0, has_side_effects=True, vmem_limit_bytes=56 * 1024 * 1024
        ),
    )(
        injection,
        used_rows,
        lodf,
        limits[:, None],
        monitored[:, None],
        outages[None, :],
        keep,
        generation,
        cost_quad[None, :],
    )


def solution(mesh):
    placed = (
        P(None, "bus"),
        P(None, "bus"),
        P(),
        P("line", "bus"),
        P("line", None),
        P("line"),
        P("line"),
        P(),
        P("bus"),
    )
    return jax.shard_map(
        functools.partial(on_device, mesh.shape["bus"], mesh.shape["line"]),
        mesh=mesh,
        in_specs=placed,
        out_specs=(P("line", "bus"), P("bus", None), P("bus", None)),
        check_vma=False,
    )
```

time: 397 us -> 203 us (0.51)
  waiting for transfers between devices: 243 us -> 0 us
  Pallas kernels: 0 us -> 160 us
  other arithmetic: 76.8 us -> 6.2 us
  matrix products: 37.6 us -> 16.9 us
  between operations: 13.9 us -> 0.69 us
    pallas_call x0 -> x1, Pallas kernels: none -> 160 us  [on_device(): pl.pallas_call(functools.partial(step_kernel, n_bus, n_line), out_shape=(...]
    reduce_scatter x2 -> x0, waiting for transfers between devices: 108 us -> none  [the longest x1 64.9 us: on_device(): lax.psum_scatter(lax.dot_general(inputs, used_rows, (((1,), (1,)), ((), (...]
    all_gather x1 -> x0, waiting for transfers between devices: 71.8 us -> none  [on_device(): all_adjoint = lax.all_gather(adjoint_half, 'bus', axis=0, tiled=True)]
    psum x2 -> x0, waiting for transfers between devices: 63 us -> none  [the longest x1 31.7 us: on_device(): outflow = lax.psum(compact[:, monitor_count:], 'line')]
    reduce_sum x16 -> x0, other arithmetic: 35.1 us -> none  [contingency(): direct = jnp.sum(raw_slope, axis=2) / outage_total]
    dot_general x16 -> x0, other arithmetic: 33.5 us -> none  [contingency(): jnp.einsum('smk,mk->sk', raw_slope, lodf, precision=lax.Precision.HIGHEST)]
    dot_general x5 -> x2, matrix products: 37.6 us -> 16.9 us  [the longest x1 13.5 us: on_device(): jnp.dot(picker, ptdf, preferred_element_type=jnp.float32)]
    concatenate x0 -> x1, other arithmetic: none -> 4 us  [on_device(): used_rows = jnp.concatenate([watched_rows, outage_rows], axis=0)]
  transfers between devices with their start and end apart: 5 -> 0, of which waited for: 5 -> 0; matrix products, arithmetic and copies ran while one was open for 0% -> 0% of each run, Pallas kernels for 0% -> 0%
where the time goes in v1:
time: 203 us
  Pallas kernels  160 us (79%)
  local copies, waits for them, and re-layouts  19.1 us (9%)
  matrix products  16.9 us (8%)
  other arithmetic  6.2 us (3%)
    pallas_call x1, Pallas kernels, on_device(): pl.pallas_call(functools.partial(step_kernel, n_bus, n_line), out_shape=(...  160 us
    dot_general x1, matrix products, on_device(): jnp.dot(picker, ptdf, preferred_element_type=jnp.float32)  13.5 us
    gather x1, local copies, waits for them, and re-layouts, on_device(): watched_rows = jnp.take(ptdf, local_monitored, axis=0, mode='clip')  12.5 us
    unnamed x13, local copies, waits for them, and re-layouts  5.04 us

profile of v1, /device:TPU:30, one launch (start us, length us, event | category | flops | bytes accessed | tf_op | source)
XLA Modules:
  0.0 202.8 jit_solution(12091282532623244600)
XLA Ops:
  0.6 0.0 copy-start
  0.6 0.9 compare_reduce_fusion
  1.6 1.3 and_convert_fusion
  2.8 0.0 copy-start.2
  2.8 13.5 %fusion.2 = bf16[512,2048]{1,0:T(8,128)(2,1)} fusion(bf16[4096,2048]{1,0:T(8,128)(2,1)} %param.12, s32[512]{0:T(512)S(1)} %get-tuple-element.4), kind=kOutput, calls=%fused_computation.6 | convolution fusion | flops 8593080320 | bytes 18876416 | tf_op jit(solution)/shard_map/dot_general | solution.py:317
  16.3 0.0 copy-done.2
  16.4 12.5 %gather_fusion = bf16[384,2048]{1,0:T(8,128)(2,1)S(1)} fusion(bf16[4096,2048]{1,0:T(8,128)(2,1)} %param.12, s32[1024]{0:T(1024)S(1)} %pad_clamp_fusion), kind=kCustom, calls=%fused_computation | custom fusion | bytes 3147264 | tf_op jit(solution)/shard_map/jit(_take)/gather | solution.py:316
  28.9 0.0 copy-start.1
  28.9 0.0 copy-start.3
  28.9 4.0 %pad_maximum_fusion.rows_ref = bf16[896,2048]{1,0:T(8,128)(2,1)} fusion(bf16[512,2048]{1,0:T(8,128)(2,1)} %fusion.2, bf16[384,2048]{1,0:T(8,128)(2,1)S(1)} %gather_fusion), kind=kLoop, calls=%fused_computation.5 | loop fusion | flops 7340032 | bytes 7340032 | tf_op jit(solution)/shard_map/concatenate | solution.py:318
  32.9 0.0 copy-start.4
  32.9 0.0 copy-done
  32.9 0.0 copy-done.1
  32.9 0.0 copy-done.3
  32.9 3.4 %subtract_convert_fusion.inj_ref = bf16[512,2048]{1,0:T(8,128)(2,1)} fusion(bf16[512,2048]{1,0:T(8,128)(2,1)S(1)} %copy-done.1, f32[24,2048]{1,0:T(8,128)S(1)} %copy-done, s32[512]{0:T(512)S(1)} %copy-done.3), kind=kOutput, calls=%fused_computation.4 | convolution fusion | flops 305147904 | bytes 4392960 | tf_op jit(solution)/shard_map/dot_general | solution.py:306
  36.3 0.0 copy-done.4
  36.3 0.8 broadcast_in_dim.35.limits_ref
  37.1 0.8 broadcast_in_dim.36.monitored_ref
  37.9 159.9 %shard_map.112 = (bf16[128,2048]{1,0:T(8,128)(2,1)}, f32[64,512]{1,0:T(8,128)}, f32[64,512]{1,0:T(8,128)}) custom-call(bf16[512,2048]{1,0:T(8,128)(2,1)} %subtract_convert_fusion.inj_ref, bf16[896,2048]{1,0:T(8,128)(2,1)} %pad_maximum_fusion.rows_ref, f32[384,512]{1,0:T(8,128)} %lodf_ref.1, f32[384,1]{1,0:T(8,128)} %broadcast_in_dim.35.limits_ref, ...), custom_call_target="tpu_custom_call" | custom-call | tf_op jit(solution)/shard_map/pallas_call | solution.py:331
  197.8 1.9 copy.19
  199.7 1.6 copy.20
  201.2 1.6 copy.21
  (2 shorter events, 0.0 us)
Async XLA Ops:
  0.6 32.3 %copy-start = (f32[24,2048]{1,0:T(8,128)S(1)}, f32[24,2048]{1,0:T(8,128)}, u32[]{:S(2)}) copy-start(f32[24,2048]{1,0:T(8,128)} %param.10) | copy-start | bytes 589828
  2.8 13.5 %copy-start.2 = (s32[384]{0:T(512)S(1)}, s32[384]{0:T(512)}, u32[]{:S(2)}) copy-start(s32[384]{0:T(512)} %param.15) | copy-start | bytes 4612
  28.9 4.0 %copy-start.1 = (bf16[512,2048]{1,0:T(8,128)(2,1)S(1)}, bf16[512,2048]{1,0:T(8,128)(2,1)}, u32[]{:S(2)}) copy-start(bf16[512,2048]{1,0:T(8,128)(2,1)} %generation_ref.1) | copy-start | bytes 6291460
  28.9 4.0 %copy-start.3 = (s32[512]{0:T(512)S(1)}, s32[512]{0:T(512)}, u32[]{:S(2)}) copy-start(s32[512]{0:T(512)} %param.11) | copy-start | bytes 6148
  32.9 3.4 %copy-start.4 = (f32[384]{0:T(512)S(1)}, f32[384]{0:T(512)}, u32[]{:S(2)}) copy-start(f32[384]{0:T(512)} %param.14) | copy-start | bytes 4612

commit v2 on v1

--- a/solution.py
+++ b/solution.py
@@ -47,9 +47,10 @@
     mon_got,
     outbus_got,
     out_all,
-    base_t,
+    base_parts,
     limit_wide,
-    direct_t,
+    wide,
+    direct_tall,
     flow2,
     sens_tall,
     sens_part,
@@ -154,7 +155,21 @@
     for d in range(1, n_bus):
         base = base + mon_got[d - 1]
     spread = jnp.concatenate([2.0 * base, jnp.zeros((LANES - own, count_m), jnp.float32)], axis=0)
-    base_t[...] = spread.T
+    turned = spread.T
+    head = turned.astype(jnp.bfloat16)
+    rest = turned - head.astype(jnp.float32)
+    middle = rest.astype(jnp.bfloat16)
+    tail = (rest - middle.astype(jnp.float32)).astype(jnp.bfloat16)
+    base_parts[...] = jnp.concatenate([head, middle, tail], axis=1)
+
+    def widen(s, carry):
+        row = lax.broadcasted_iota(jnp.int32, (3 * LANES, LANES), 0)
+        chosen = (row == s) | (row == s + LANES) | (row == s + 2 * LANES)
+        selector = jnp.where(chosen, 1.0, 0.0).astype(jnp.bfloat16)
+        wide[s] = jnp.dot(base_parts[...], selector, preferred_element_type=jnp.float32)
+        return carry
+
+    lax.fori_loop(0, own, widen, 0, unroll=2)
     for copy in ob_copies:
         copy.wait()
     flow = out_sum[own_rows, :]
@@ -169,19 +184,16 @@
         )
         copy.start()
         oa_copies.append(copy)
-    direct_t[...] = jnp.zeros_like(direct_t)
     for copy in oa_copies:
         copy.wait()
     flows = jnp.concatenate([out_all[j] for j in range(n_line)], axis=1)
     outflow_ref[...] = flows
     flow2[...] = jnp.broadcast_to((2.0 * flows)[:, None, :], flow2.shape)
 
-    lane = lax.broadcasted_iota(jnp.int32, (8, LANES), 1)
     group = 8
     k_tiles = count_k // LANES
 
     def one_scenario(s, carry):
-        mine = lane == s
         flow_rows = [
             flow2[s, :, t * LANES : (t + 1) * LANES] for t in range(k_tiles)
         ]
@@ -191,7 +203,7 @@
             for i in range(group):
                 start = pl.multiple_of((g * group + i) * 8, 8)
                 here = pl.ds(start, 8)
-                column = jnp.sum(jnp.where(mine, base_t[here, :], 0.0), axis=1, keepdims=True)
+                column = wide[s, here, :]
                 limit = limit_wide[here, :]
                 low = column - limit
                 high = column + limit
@@ -202,8 +214,7 @@
                     slope = jnp.tanh(change + low) + jnp.tanh(change + high)
                     along = along + slope
                     sums[t] = sums[t] + factor * slope
-                direct = jnp.sum(along, axis=1, keepdims=True)
-                direct_t[here, :] = jnp.where(mine, direct, direct_t[here, :])
+                wide[s, here, :] = along
             return tuple(sums)
 
         sums = lax.fori_loop(
@@ -227,7 +238,19 @@
         )
         copy.start()
         se_copies.append(copy)
-    direct = direct_t[...].T[:own, :] * (0.5 / count_k)
+    ones = jnp.ones((16, 2 * LANES), jnp.bfloat16)
+
+    def add_lanes(s, carry):
+        along = wide[s]
+        head = along.astype(jnp.bfloat16)
+        rest = (along - head.astype(jnp.float32)).astype(jnp.bfloat16)
+        both = jnp.concatenate([head, rest], axis=1)
+        sums = lax.dot_general(ones, both, ROWS_DOT, preferred_element_type=jnp.float32)
+        direct_tall[s] = sums[:8, :]
+        return carry
+
+    lax.fori_loop(0, own, add_lanes, 0, unroll=2)
+    direct = jnp.sum(direct_tall[...], axis=1) * (0.0625 / count_k)
     match = (monitored_ref[...] == outages_ref[...]).astype(jnp.float32)
     for copy in se_copies:
         copy.wait()
@@ -294,6 +317,39 @@
     for d in range(1, n_hi):
         total = total + hi_got[d - 1].astype(jnp.float32)
     gradient_ref[...] = total.astype(jnp.bfloat16)
+
+
+def pick_kernel(ids_ref, ptdf_ref, rows_ref, picker):
+    used, lines = picker.shape
+
+    @pl.when(pl.program_id(0) == 0)
+    def _():
+        ids = ids_ref[...]
+        for start in range(0, lines, 512):
+            place = start + lax.broadcasted_iota(jnp.int32, (used, 512), 1)
+            picker[:, start : start + 512] = jnp.where(ids == place, 1.0, 0.0).astype(jnp.bfloat16)
+
+    rows_ref[...] = jnp.dot(
+        picker[...], ptdf_ref[...], preferred_element_type=jnp.float32
+    ).astype(jnp.bfloat16)
+
+
+def pick_rows(ids, ptdf):
+    lines, buses = ptdf.shape
+    used = ids.shape[0]
+    block = 256
+    return pl.pallas_call(
+        pick_kernel,
+        grid=(buses // block,),
+        out_shape=jax.ShapeDtypeStruct((used, buses), jnp.bfloat16),
+        in_specs=[
+            pl.BlockSpec((used, 1), lambda i: (0, 0)),
+            pl.BlockSpec((lines, block), lambda i: (0, i)),
+        ],
+        out_specs=pl.BlockSpec((used, block), lambda i: (0, i)),
+        scratch_shapes=[pltpu.VMEM((used, lines), jnp.bfloat16)],
+        compiler_params=pltpu.CompilerParams(vmem_limit_bytes=48 * 1024 * 1024),
+    )(ids[:, None], ptdf)
 
 
 def on_device(
@@ -310,12 +366,8 @@
     count_m, count_k = lodf.shape
     first_line = lax.axis_index("line") * line_rows
     local_outages = outages - first_line
-    local_monitored = monitored - first_line
-    positions = jnp.arange(line_rows, dtype=jnp.int32)
-    picker = (local_outages[:, None] == positions[None, :]).astype(jnp.bfloat16)
-    watched_rows = jnp.take(ptdf, local_monitored, axis=0, mode="clip")
-    outage_rows = jnp.dot(picker, ptdf, preferred_element_type=jnp.float32).astype(jnp.bfloat16)
-    used_rows = jnp.concatenate([watched_rows, outage_rows], axis=0)
+    local_used = jnp.concatenate([monitored - first_line, local_outages])
+    used_rows = pick_rows(local_used, ptdf)
     seen = jnp.any(monitored[:, None] == outages[None, :], axis=0)
     keep = (local_outages >= 0) & (local_outages < line_rows) & jnp.logical_not(seen)
     keep = keep.astype(jnp.float32)[None, :]
@@ -345,9 +397,10 @@
             pltpu.VMEM((n_bus - 1, own, count_m), f32),
             pltpu.VMEM((n_bus - 1, own, width), f32),
             pltpu.VMEM((n_line, own, width), f32),
+            pltpu.VMEM((count_m, 3 * LANES), bf16),
             pltpu.VMEM((count_m, LANES), f32),
-            pltpu.VMEM((count_m, LANES), f32),
-            pltpu.VMEM((count_m, LANES), f32),
+            pltpu.VMEM((own, count_m, LANES), f32),
+            pltpu.VMEM((own, 8, count_m), f32),
             pltpu.VMEM((own, 8, count_k), f32),
             pltpu.VMEM((own, 8, count_k), f32),
             pltpu.VMEM((own, count_k), f32),
@@ -376,7 +429,7 @@
             dma((n_hi - 1,)),
         ],
         compiler_params=pltpu.CompilerParams(
-            collective_id=0, has_side_effects=True, vmem_limit_bytes=56 * 1024 * 1024
+            collective_id=0, has_side_effects=True, vmem_limit_bytes=58 * 1024 * 1024
         ),
     )(
         injection,

time: 203 us -> 152 us (0.75)
  Pallas kernels: 160 us -> 133 us
  matrix products: 16.9 us -> 4.91 us
  local copies, waits for them, and re-layouts: 19.1 us -> 9.92 us
  other arithmetic: 6.2 us -> 2.88 us
    pallas_call x1, Pallas kernels: 160 us -> 114 us  [on_device(): pl.pallas_call(functools.partial(step_kernel, n_bus, n_line), out_shape=(...]
    pallas_call x0 -> x1, Pallas kernels: none -> 19.7 us  [pick_rows(): pl.pallas_call(pick_kernel, grid=(buses // block,), out_shape=jax.ShapeDt...]
    dot_general x1 -> x0, matrix products: 13.5 us -> none  [on_device(): jnp.dot(picker, ptdf, preferred_element_type=jnp.float32)]
    gather x1 -> x0, local copies, waits for them, and re-layouts: 12.5 us -> none  [on_device(): watched_rows = jnp.take(ptdf, local_monitored, axis=0, mode='clip')]
    concatenate x1, other arithmetic: 4 us -> 0.01 us  [on_device(): local_used = jnp.concatenate([monitored - first_line, local_outages])]
    unnamed x13 -> x7, local copies, waits for them, and re-layouts: 5.04 us -> 6.8 us
where the time goes in v2:
time: 152 us
  Pallas kernels  133 us (88%)
  local copies, waits for them, and re-layouts  9.92 us (7%)
  matrix products  4.91 us (3%)
  other arithmetic  2.88 us (2%)
    pallas_call x1, Pallas kernels, on_device(): pl.pallas_call(functools.partial(step_kernel, n_bus, n_line), out_shape=(...  114 us
    pallas_call x1, Pallas kernels, pick_rows(): pl.pallas_call(pick_kernel, grid=(buses // block,), out_shape=jax.ShapeDt...  19.7 us
    unnamed x7, local copies, waits for them, and re-layouts  6.8 us
    dot_general x1, matrix products, on_device(): loads = jnp.dot(profile_pick, profiles, precision=HIGH)  4.91 us

profile of v2, /device:TPU:30, one launch (start us, length us, event | category | flops | bytes accessed | tf_op | source)
XLA Modules:
  0.0 151.9 jit_solution(15152125232898129211)
XLA Ops:
  0.6 0.0 copy-start
  0.6 0.9 compare_reduce_fusion
  1.6 0.7 broadcast_subtract_fusion.1
  2.3 1.3 and_convert_fusion
  3.5 1.5 broadcast_in_dim.33.limits_ref
  5.0 1.5 broadcast_in_dim.34.monitored_ref
  6.5 0.2 broadcast_in_dim.32.ids_ref
  6.7 0.0 copy-done
  6.7 4.9 %subtract_convert_fusion.inj_ref = bf16[512,2048]{1,0:T(8,128)(2,1)} fusion(bf16[512,2048]{1,0:T(8,128)(2,1)} %generation_ref.1, f32[24,2048]{1,0:T(8,128)S(1)} %copy-done, s32[512]{0:T(512)} %param.11), kind=kOutput, calls=%fused_computation | convolution fusion | flops 305147904 | bytes 4392960 | tf_op jit(solution)/shard_map/dot_general | solution.py:362
  11.6 19.7 %shard_map.112.rows_ref = bf16[896,2048]{1,0:T(8,128)(2,1)S(1)} custom-call(s32[896,1]{1,0:T(8,128)S(1)} %broadcast_in_dim.32.ids_ref, bf16[4096,2048]{1,0:T(8,128)(2,1)} %ptdf_ref.1), custom_call_target="tpu_custom_call" | custom-call | tf_op jit(solution)/shard_map/pallas_call | solution.py:341
  31.3 0.0 copy-start.1
  31.3 1.8 %copy-done.1 = bf16[896,2048]{1,0:T(8,128)(2,1)} copy-done((bf16[896,2048]{1,0:T(8,128)(2,1)}, bf16[896,2048]{1,0:T(8,128)(2,1)S(1)}, u32[]{:S(2)}) %copy-start.1) | copy-done | bytes 3670040
  33.1 113.8 %shard_map.113 = (bf16[128,2048]{1,0:T(8,128)(2,1)}, f32[64,512]{1,0:T(8,128)}, f32[64,512]{1,0:T(8,128)}) custom-call(bf16[512,2048]{1,0:T(8,128)(2,1)} %subtract_convert_fusion.inj_ref, bf16[896,2048]{1,0:T(8,128)(2,1)} %copy-done.1, f32[384,512]{1,0:T(8,128)} %lodf_ref.1, f32[384,1]{1,0:T(8,128)} %broadcast_in_dim.33.limits_ref, ...), custom_call_target="tpu_custom_call" | custom-call | tf_op jit(solution)/shard_map/pallas_call | solution.py:383
  146.9 1.9 %copy.21 = bf16[128,2048]{1,0:T(8,128)(2,1)} copy(bf16[128,2048]{1,0:T(8,128)(2,1)} %get-tuple-element.8) | data formatting | bytes 1048576
  148.8 1.6 %copy.22 = f32[64,512]{1,0:T(8,128)} copy(f32[64,512]{1,0:T(8,128)} %get-tuple-element.9) | data formatting | bytes 262144
  150.3 1.6 %copy.23 = f32[64,512]{1,0:T(8,128)} copy(f32[64,512]{1,0:T(8,128)} %get-tuple-element.10) | data formatting | bytes 262144
  (1 shorter events, 0.0 us)
Async XLA Ops:
  0.6 6.0 %copy-start = (f32[24,2048]{1,0:T(8,128)S(1)}, f32[24,2048]{1,0:T(8,128)}, u32[]{:S(2)}) copy-start(f32[24,2048]{1,0:T(8,128)} %param.10) | copy-start | bytes 589828
  31.3 1.8 %copy-start.1 = (bf16[896,2048]{1,0:T(8,128)(2,1)}, bf16[896,2048]{1,0:T(8,128)(2,1)S(1)}, u32[]{:S(2)}) copy-start(bf16[896,2048]{1,0:T(8,128)(2,1)S(1)} %shard_map.112.rows_ref) | copy-start | bytes 11010052
